TPU v7x, 32 devices: a whole 2x2x4 slice. The times are simulated.
32 devices in a mesh: groups: 1, frame: 4 (over y, x), row: 8 (over z, core).
Axes of the slice: x: 2, y: 2, z: 4, core: 2. Of those that a mesh axis runs over, the one named last changes fastest.
Arguments:
- layer_input: bfloat16 [4096, 3072], P(('groups', 'frame', 'row')), may hold values from -6 to 6
- queries: bfloat16 [4096, 3072], P(('groups', 'frame', 'row')), may hold values from -64 to 64
- key_input: bfloat16 [4096, 3072], P(('groups', 'frame', 'row')), may hold values from -4.5 to 4.5
- values: bfloat16 [4096, 3072], P(('groups', 'frame', 'row')), may hold values from -6 to 6
- key_tiles: int32 [32, 5], P(('groups', 'frame', 'row')), may hold values from -1 to 31, as said below
- expert_ids: int32 [4096, 2], P(('groups', 'frame', 'row')), may hold values from 0 to 3, all different within a row; in each aligned block of 128 rows (0 to 127, 128 to 255, ...) at most 128 rows name the same one
- norm_gain: float32 [3072], replicated, may hold values from 0.5 to 1.5
- router: bfloat16 [3072, 4], replicated, may hold values from -0.109375 to 0.109375
- w_up: bfloat16 [8, 3072, 768], P('row'), may hold values from -0.109375 to 0.109375
- w_down: bfloat16 [8, 768, 3072], P('row'), may hold values from -0.15625 to 0.15625
Outputs:
- layer_output: bfloat16 [4096, 3072], P(('groups', 'frame', 'row'))
Inputs may be any that keep to these rules, and one draw needn't show every extreme that they name: `key_tiles`: entry 0 of row t is t. Then come, in any order, distinct tiles among the up to four whose frame position or row position differs from t's by one while the other is the same; the remaining entries are -1. Some tile lists all four. `expert_ids`: each row names two different experts. Within the rows of one device no expert is named more than 128 times, and in every draw some expert is named exactly 128 times there.
All inputs are finite; a program needn't handle non-finite values.
Results may differ from a plain program's by a relative error of at most 0.007.
Values may be sent and summed in bfloat16 or wider, within the bound.
A program may use at most 128 MiB of HBM per device.

v0:
```python
import jax
import jax.numpy as jnp
from jax import lax
from jax.sharding import PartitionSpec as P

HEADS = 24
TILE = 128


def shifted(value, axis, steps):
    count = lax.axis_size(axis)
    initial, last = (max(0, -steps), min(count, count - steps))
    return lax.ppermute(value, axis, [(source, source + steps) for source in range(initial, last)])


def with_halo(block, sides, width):
    for axis, dim in sides:
        count = lax.axis_size(axis)
        forward = [(i, i + 1) for i in range(count - 1)]
        backward = [(target, source) for source, target in forward]
        low = lax.ppermute(
            lax.slice_in_dim(block, block.shape[dim] - width, None, axis=dim), axis, forward
        )
        high = lax.ppermute(lax.slice_in_dim(block, 0, width, axis=dim), axis, backward)
        block = jnp.concatenate([low, block, high], axis=dim)
    return block


def tile_partials(query_rows, key_rows, value_rows, head_count):
    batches, row_count, features = query_rows.shape
    head_size = features // head_count
    query_split = query_rows.reshape(batches, row_count, head_count, head_size)
    key_split = key_rows.reshape(batches, -1, head_count, head_size)
    value_split = value_rows.reshape(batches, -1, head_count, head_size)
    scores = jnp.einsum(
        "bqhd,bkhd->bhqk", query_split, key_split, preferred_element_type=jnp.float32
    ) * head_size ** (-0.5)
    maxima = jnp.max(scores, axis=-1)
    expos = jnp.exp(scores - maxima[..., None])
    totals = jnp.sum(expos, axis=-1)
    mixed = jnp.einsum(
        "bhqk,bkhd->bqhd",
        expos.astype(jnp.bfloat16),
        value_split,
        preferred_element_type=jnp.float32,
    )
    mixed = mixed / jnp.transpose(totals, (0, 2, 1))[..., None]
    return (mixed.reshape(batches, row_count, features).astype(jnp.bfloat16), maxima, totals)


def merge_partials(partial_value, maxima, totals, listed, head_count):
    masked = jnp.where(listed[:, :, None, None], maxima, -jnp.inf)
    peak_value = jnp.max(masked, axis=1, keepdims=True)
    weights = totals * jnp.exp(masked - peak_value)
    weight_sum = jnp.sum(weights, axis=1)
    tiles_here, cands, row_count, features = partial_value.shape
    split = partial_value.reshape(tiles_here, cands, row_count, head_count, features // head_count)
    scaled = jnp.sum(split * jnp.transpose(weights, (0, 1, 3, 2))[..., None], axis=1)
    merged = scaled / jnp.transpose(weight_sum, (0, 2, 1))[..., None]
    return merged.reshape(tiles_here, row_count, features)


def frame_return(part_out, part_max, part_sum, offset):
    return (
        shifted(part_out.astype(jnp.float32), "frame", offset).astype(part_out.dtype),
        shifted(part_max, "frame", offset),
        shifted(part_sum, "frame", offset),
    )


def row_return(part_out, part_max, part_sum, offset):
    return (
        shifted(part_out.astype(jnp.float32), "row", offset).astype(part_out.dtype),
        shifted(part_max, "row", offset),
        shifted(part_sum, "row", offset),
    )


def half_expert(token_rows, w_up, w_down):
    up_part = jnp.dot(token_rows, w_up[0], preferred_element_type=jnp.float32)
    inner = jax.nn.gelu(up_part, approximate=True).astype(jnp.bfloat16)
    return jnp.dot(inner, w_down[0], preferred_element_type=jnp.float32).astype(jnp.bfloat16)


def local(
    layer_input, queries, key_input, values, key_tiles, expert_ids, norm_gain, router, w_up, w_down
):
    head_count = HEADS
    tile_rows = TILE
    per_device = key_tiles.shape[0]
    features = layer_input.shape[1]
    frame_index = lax.axis_index("frame")
    row_index = lax.axis_index("row")
    frame_count = lax.axis_size("frame")
    row_count = lax.axis_size("row")
    row_tiles = row_count * per_device
    query_tiles = queries.reshape(per_device, tile_rows, features)
    extended = with_halo(query_tiles[None], (("frame", 0), ("row", 1)), 1)
    middle = extended[1]
    visitors = jnp.stack(
        [
            query_tiles,
            extended[0, 1 : per_device + 1],
            extended[2, 1 : per_device + 1],
            middle[0:per_device],
            middle[2 : per_device + 2],
        ]
    )
    own_keys = jnp.broadcast_to(
        key_input.reshape(1, per_device, tile_rows, features), (5, per_device, tile_rows, features)
    )
    own_values = jnp.broadcast_to(
        values.reshape(1, per_device, tile_rows, features), (5, per_device, tile_rows, features)
    )
    flat_shape = (5 * per_device, tile_rows, features)
    partial_value, maxima, totals = tile_partials(
        visitors.reshape(flat_shape),
        own_keys.reshape(flat_shape),
        own_values.reshape(flat_shape),
        head_count,
    )
    partial_value = partial_value.reshape(5, per_device, tile_rows, features)
    maxima = maxima.reshape(5, per_device, head_count, tile_rows)
    totals = totals.reshape(5, per_device, head_count, tile_rows)
    from_lower = frame_return(partial_value[2], maxima[2], totals[2], 1)
    from_upper = frame_return(partial_value[1], maxima[1], totals[1], -1)
    below_edge = row_return(partial_value[4], maxima[4], totals[4], 1)
    above_edge = row_return(partial_value[3], maxima[3], totals[3], -1)
    local_sets = (partial_value, maxima, totals)
    from_below = tuple(
        (
            jnp.concatenate([below_edge[member], local_sets[member][4][: per_device - 1]], axis=0)
            for member in range(3)
        )
    )
    from_above = tuple(
        (
            jnp.concatenate([local_sets[member][3][1:], above_edge[member]], axis=0)
            for member in range(3)
        )
    )
    pieces = [
        (partial_value[0], maxima[0], totals[0]),
        from_lower,
        from_upper,
        from_below,
        from_above,
    ]
    partial_value = jnp.stack([piece[0].astype(jnp.float32) for piece in pieces], axis=1)
    maxima = jnp.stack([piece[1] for piece in pieces], axis=1)
    totals = jnp.stack([piece[2] for piece in pieces], axis=1)
    local_tiles = jnp.arange(per_device, dtype=jnp.int32)
    row_pos = row_index * per_device + local_tiles
    tile_id = frame_index * row_tiles + row_pos
    cand_ids = jnp.stack(
        [tile_id, tile_id - row_tiles, tile_id + row_tiles, tile_id - 1, tile_id + 1], axis=1
    )
    inside = jnp.stack(
        [
            jnp.ones((per_device,), bool),
            jnp.broadcast_to(frame_index >= 1, (per_device,)),
            jnp.broadcast_to(frame_index < frame_count - 1, (per_device,)),
            row_pos >= 1,
            row_pos < row_tiles - 1,
        ],
        axis=1,
    )
    listed = inside & jnp.any(key_tiles[:, :, None] == cand_ids[:, None, :], axis=1)
    attended = merge_partials(partial_value, maxima, totals, listed, head_count)
    hidden_state = layer_input.astype(jnp.float32) + attended.reshape(-1, features)
    mean_square = jnp.mean(hidden_state * hidden_state, axis=1, keepdims=True)
    normed = (hidden_state * lax.rsqrt(mean_square + 1e-06) * norm_gain).astype(jnp.bfloat16)
    logits = jnp.dot(normed, router, preferred_element_type=jnp.float32)
    token_count = normed.shape[0]
    expert_count = router.shape[1]
    capacity = min(token_count, max(2, 4 * token_count // expert_count))
    expert_range = jnp.arange(expert_count, dtype=jnp.int32)
    selector = expert_ids[:, :, None] == expert_range[None, None, :]
    gates = jax.nn.sigmoid(jnp.sum(logits[:, None, :] * selector.astype(jnp.float32), axis=2))
    onehot = selector.astype(jnp.int32).reshape(token_count * 2, expert_count)
    earlier = jnp.cumsum(onehot, axis=0) - onehot
    slot_index = jnp.sum(earlier * onehot, axis=1)
    flat_ids = expert_ids.reshape(-1)
    doubled = jnp.repeat(normed, 2, axis=0)
    outgoing = (
        jnp.zeros((expert_count, capacity, features), jnp.bfloat16)
        .at[flat_ids, slot_index]
        .set(doubled)
    )
    padded_out = jnp.repeat(outgoing, 2, axis=0)
    arrived = lax.all_to_all(padded_out, "row", split_axis=0, concat_axis=0, tiled=True)
    result = half_expert(arrived.reshape(-1, features), w_up, w_down)
    returned = lax.all_to_all(
        result.reshape(arrived.shape), "row", split_axis=0, concat_axis=0, tiled=True
    )
    halves = returned.reshape(expert_count, 2, capacity, features)
    both = halves[:, 0].astype(jnp.float32) + halves[:, 1].astype(jnp.float32)
    picked = both[flat_ids, slot_index].reshape(token_count, 2, features)
    return (hidden_state + jnp.sum(gates[:, :, None] * picked, axis=1)).astype(jnp.bfloat16)


def solution(mesh):
    return jax.shard_map(
        local,
        mesh=mesh,
        in_specs=(
            P(("groups", "frame", "row"), None),
            P(("groups", "frame", "row"), None),
            P(("groups", "frame", "row"), None),
            P(("groups", "frame", "row"), None),
            P(("groups", "frame", "row"), None),
            P(("groups", "frame", "row"), None),
            P(),
            P(),
            P("row", None, None),
            P("row", None, None),
        ),
        out_specs=P(("groups", "frame", "row"), None),
        check_vma=False,
    )
```

profile of v0, /device:TPU:4, one launch (start us, length us, event | category | flops | bytes accessed | tf_op | source)
XLA Modules:
  0.0 552.8 jit_solution(9421253526194366750)
XLA Ops:
  0.0 1.6 copy.57
  1.6 3.4 collective-permute-start
  5.0 3.3 collective-permute-start.1
  8.4 16.5 %collective-permute-done = bf16[1,1,128,3072]{2,3,1,0:T(8,128)(2,1)S(1)} collective-permute-done((bf16[1,1,128,3072]{2,3,1,0:T(8,128)(2,1)S(1)}, bf16[1,1,128,3072]{2,3,1,0:T(8,128)(2,1)S(1)}, u32[]{:S(2)}, u32[]{:S(2)}) %collective-permute-start) | collective-permute-done | bytes 786464 | tf_op jit(solution)/shard_map/ppermute | solution.py:21
  24.8 13.8 %collective-permute-done.1 = bf16[1,1,128,3072]{2,3,1,0:T(8,128)(2,1)S(1)} collective-permute-done((bf16[1,1,128,3072]{2,3,1,0:T(8,128)(2,1)S(1)}, bf16[1,1,128,3072]{2,3,1,0:T(8,128)(2,1)S(1)}, u32[]{:S(2)}, u32[]{:S(2)}) %collective-permute-start.1) | collective-permute-done | bytes 786464 | tf_op jit(solution)/shard_map/ppermute | solution.py:24
  38.7 1.7 pad_maximum_fusion
  40.3 2.8 collective-permute-start.2
  43.1 1.3 collective-permute-start.3
  44.9 1.2 copy.59
  46.1 2.3 copy.77
  48.4 1.2 reduce-window.6
  50.4 2.1 constant_dynamic-update-slice_fusion.4
  55.4 1.2 slice.115
  57.0 1.2 slice.116
  60.5 5.0 multiply_reduce_fusion.1
  65.6 2.4 fusion.1
  68.0 2.5 fusion
  70.9 1.9 collective-permute-start.12
  72.8 5.3 collective-permute-start.13
  78.1 19.0 %collective-permute-start.14 = (f32[1,24,128]{2,1,0:T(8,128)S(1)}, f32[1,24,128]{2,1,0:T(8,128)S(1)}, u32[]{:S(2)}, u32[]{:S(2)}) collective-permute-start(f32[1,24,128]{2,1,0:T(8,128)S(1)} %get-tuple-element.14), channel_id=1, source_target_pairs={{0,1},{1,2},{2,3},{3,4},{4,5},{5,6},{6,7},{8,9},{9,10},{10,11},{11... | collective-permute-start | bytes 36872 | tf_op jit(solution)/shard_map/ppermute | solution.py:13
  97.1 1.3 collective-permute-start.15
  98.4 1.9 collective-permute-start.8
  100.3 4.8 collective-permute-start.9
  105.2 2.5 collective-permute-start.10
  107.7 1.3 collective-permute-start.11
  109.0 1.9 collective-permute-start.4
  111.0 4.8 collective-permute-start.5
  115.8 3.9 collective-permute-start.6
  119.8 1.5 collective-permute-start.7
  121.5 9.1 %collective-permute-done.4 = bf16[1,128,3072]{1,2,0:T(8,128)(2,1)S(1)} collective-permute-done((bf16[1,128,3072]{1,2,0:T(8,128)(2,1)S(1)}, bf16[1,128,3072]{1,2,0:T(8,128)(2,1)S(1)}, u32[]{:S(2)}, u32[]{:S(2)}) %collective-permute-start.4) | collective-permute-done | bytes 786464 | tf_op jit(solution)/shard_map/ppermute | solution.py:13
  130.7 13.1 %collective-permute-done.5 = bf16[1,128,3072]{1,2,0:T(8,128)(2,1)S(1)} collective-permute-done((bf16[1,128,3072]{1,2,0:T(8,128)(2,1)S(1)}, bf16[1,128,3072]{1,2,0:T(8,128)(2,1)S(1)}, u32[]{:S(2)}, u32[]{:S(2)}) %collective-permute-start.5) | collective-permute-done | bytes 786464 | tf_op jit(solution)/shard_map/ppermute | solution.py:13
  144.2 1.1 multiply_reduce_fusion
  145.3 1.3 broadcast_divide_fusion
  146.7 1.9 copy.67
  149.2 2.0 broadcast_in_dim.33
  151.1 4.6 reshape.649
  155.7 2.0 broadcast_in_dim.32
  157.8 56.3 %scatter_fusion = bf16[4,128,3072]{2,1,0:T(8,128)(2,1)} fusion(bf16[4,128,3072]{2,1,0:T(8,128)(2,1)} %broadcast_in_dim.32, s32[256]{0:T(256)S(1)} %bitcast.138, bf16[256,3072]{1,0:T(8,128)(2,1)} %reshape.649), kind=kCustom, calls=%fused_computation.1 | custom fusion | bytes 4720640 | tf_op jit(solution)/shard_map/scatter | solution.py:188
  214.1 2.7 broadcast_in_dim.34
  216.8 147.0 %all_to_all.10 = bf16[8,128,3072]{2,1,0:T(8,128)(2,1)} all-to-all(bf16[8,128,3072]{2,1,0:T(8,128)(2,1)S(1)} %bitcast.136), channel_id=1, replica_groups=mesh['groups'=1,'frame'=4,'row'=8] {'row'}, dimensions={0} | all-to-all | bytes 12582912 | tf_op jit(solution)/shard_map/all_to_all | solution.py:191
  363.8 19.4 %convolution_convert_fusion = bf16[1024,3072]{1,0:T(8,128)(2,1)} fusion(bf16[1,768,3072]{2,1,0:T(8,128)(2,1)} %param.19, bf16[1024,3072]{1,0:T(8,128)(2,1)} %bitcast.144, bf16[1,3072,768]{2,1,0:T(8,128)(2,1)} %param.18), kind=kOutput, calls=%fused_computation.10 | convolution fusion | flops 9673900032 | bytes 22020096 | tf_op jit(solution)/shard_map/dot_general | solution.py:82
  383.2 5.1 all-to-all-start.1
  388.8 138.2 %all-to-all-done.1 = bf16[8,128,3072]{2,1,0:T(8,128)(2,1)} async-done(((bf16[8,128,3072]{2,1,0:T(8,128)(2,1)}), bf16[8,128,3072]{2,1,0:T(8,128)(2,1)}, u32[]{:S(2)}, u32[]{:S(2)}) %all-to-all-start.1) | async-done | bytes 6291488 | tf_op jit(solution)/shard_map/all_to_all | solution.py:193
  527.0 6.6 %add_bitcast_fusion = f32[4,128,3072]{2,1,0:T(8,128)} fusion(bf16[4,2,128,3072]{3,2,1,0:T(8,128)(2,1)} %bitcast.54), kind=kLoop, calls=%fused_computation.9 | loop fusion | flops 4718592 | bytes 12582912 | tf_op jit(solution)/shard_map/add | solution.py:197
  533.7 6.4 %gather_fusion = f32[256,3072]{1,0:T(8,128)} fusion(f32[4,128,3072]{2,1,0:T(8,128)} %add_bitcast_fusion, s32[256]{0:T(256)S(1)} %bitcast.137), kind=kCustom, calls=%fused_computation | custom fusion | bytes 6293504 | tf_op jit(solution)/shard_map/gather | solution.py:198
  540.0 5.2 reshape.636
  545.2 6.4 %multiply_reduce_fusion.2 = f32[128,3072]{1,0:T(8,128)S(1)} fusion(f32[128,2,3072]{2,1,0:T(2,128)} %reshape.636, f32[128,2]{1,0:T(8,128)S(1)} %copy.68), kind=kLoop, calls=%fused_computation.28 | loop fusion | flops 1179648 | bytes 4719616 | tf_op jit(solution)/shard_map/reduce_sum | solution.py:199
  551.7 1.2 add_convert_fusion
  (81 shorter events, 8.9 us)
Async XLA Ops:
  0.0 52.5 %copy-start = (bf16[128,3072]{1,0:T(8,128)(2,1)S(1)}, bf16[128,3072]{1,0:T(8,128)(2,1)}, u32[]{:S(2)}) copy-start(bf16[128,3072]{1,0:T(8,128)(2,1)} %param.12) | copy-start | bytes 2359300
  0.0 44.4 %copy-start.6 = (s32[128,2]{0,1:T(2,128)S(1)}, s32[128,2]{0,1:T(2,128)}, u32[]{:S(2)}) copy-start(s32[128,2]{0,1:T(2,128)} %param.15) | copy-start | bytes 3076
  1.6 48.6 %copy-start.7 = (s32[1,5]{1,0:T(1,128)S(1)}, s32[1,5]{1,0:T(1,128)}, u32[]{:S(2)}) copy-start(s32[1,5]{1,0:T(1,128)} %param.14) | copy-start | bytes 64
  1.6 23.2 %collective-permute-start = (bf16[1,1,128,3072]{2,3,1,0:T(8,128)(2,1)S(1)}, bf16[1,1,128,3072]{2,3,1,0:T(8,128)(2,1)S(1)}, u32[]{:S(2)}, u32[]{:S(2)}) collective-permute-start(bf16[1,1,128,3072]{2,3,1,0:T(8,128)(2,1)S(1)} %bitcast.139), channel_id=1, source_target_pairs={{0,8},{8,16},{16,24},{1,9},{9,17},{17,25},{2,10},{10,18},{18,26},{... | collective-permute-start | bytes 2359304 | tf_op jit(solution)/shard_map/ppermute | solution.py:21
  5.0 33.6 %collective-permute-start.1 = (bf16[1,1,128,3072]{2,3,1,0:T(8,128)(2,1)S(1)}, bf16[1,1,128,3072]{2,3,1,0:T(8,128)(2,1)S(1)}, u32[]{:S(2)}, u32[]{:S(2)}) collective-permute-start(bf16[1,1,128,3072]{2,3,1,0:T(8,128)(2,1)S(1)} %bitcast.140), channel_id=1, source_target_pairs={{8,0},{16,8},{24,16},{9,1},{17,9},{25,17},{10,2},{18,10},{26,18},{... | collective-permute-start | bytes 2359304 | tf_op jit(solution)/shard_map/ppermute | solution.py:24
  40.3 15.1 %collective-permute-start.2 = (bf16[3,1,128,3072]{2,3,1,0:T(8,128)(2,1)}, bf16[3,1,128,3072]{2,3,1,0:T(8,128)(2,1)}, u32[]{:S(2)}, u32[]{:S(2)}) collective-permute-start(bf16[3,1,128,3072]{2,3,1,0:T(8,128)(2,1)} %pad_maximum_fusion), channel_id=1, source_target_pairs={{0,1},{1,2},{2,3},{3,4},{4,5},{5,6},{6,7},{8,9},{9,10},{10,11},{11... | collective-permute-start | bytes 7077896 | tf_op jit(solution)/shard_map/ppermute | solution.py:21
  43.1 13.9 %collective-permute-start.3 = (bf16[3,1,128,3072]{2,3,1,0:T(8,128)(2,1)}, bf16[3,1,128,3072]{2,3,1,0:T(8,128)(2,1)}, u32[]{:S(2)}, u32[]{:S(2)}) collective-permute-start(bf16[3,1,128,3072]{2,3,1,0:T(8,128)(2,1)} %pad_maximum_fusion), channel_id=1, source_target_pairs={{1,0},{2,1},{3,2},{4,3},{5,4},{6,5},{7,6},{9,8},{10,9},{11,10},{12... | collective-permute-start | bytes 7077896 | tf_op jit(solution)/shard_map/ppermute | solution.py:24
  65.6 2.4 copy-start.3
  70.9 29.5 %collective-permute-start.12 = (f32[1,24,128]{2,1,0:T(8,128)S(1)}, f32[1,24,128]{2,1,0:T(8,128)S(1)}, u32[]{:S(2)}, u32[]{:S(2)}) collective-permute-start(f32[1,24,128]{2,1,0:T(8,128)S(1)} %get-tuple-element.16), channel_id=1, source_target_pairs={{0,8},{8,16},{16,24},{1,9},{9,17},{17,25},{2,10},{10,18},{18,26},{... | collective-permute-start | bytes 36872 | tf_op jit(solution)/shard_map/ppermute | solution.py:13
  72.8 32.4 %collective-permute-start.13 = (f32[1,24,128]{2,1,0:T(8,128)S(1)}, f32[1,24,128]{2,1,0:T(8,128)S(1)}, u32[]{:S(2)}, u32[]{:S(2)}) collective-permute-start(f32[1,24,128]{2,1,0:T(8,128)S(1)} %get-tuple-element.15), channel_id=1, source_target_pairs={{8,0},{16,8},{24,16},{9,1},{17,9},{25,17},{10,2},{18,10},{26,18},{... | collective-permute-start | bytes 36872 | tf_op jit(solution)/shard_map/ppermute | solution.py:13
  78.1 29.6 %collective-permute-start.14 = (f32[1,24,128]{2,1,0:T(8,128)S(1)}, f32[1,24,128]{2,1,0:T(8,128)S(1)}, u32[]{:S(2)}, u32[]{:S(2)}) collective-permute-start(f32[1,24,128]{2,1,0:T(8,128)S(1)} %get-tuple-element.14), channel_id=1, source_target_pairs={{0,1},{1,2},{2,3},{3,4},{4,5},{5,6},{6,7},{8,9},{9,10},{10,11},{11... | collective-permute-start | bytes 36872 | tf_op jit(solution)/shard_map/ppermute | solution.py:13
  97.1 11.9 %collective-permute-start.15 = (f32[1,24,128]{2,1,0:T(8,128)S(1)}, f32[1,24,128]{2,1,0:T(8,128)S(1)}, u32[]{:S(2)}, u32[]{:S(2)}) collective-permute-start(f32[1,24,128]{2,1,0:T(8,128)S(1)} %get-tuple-element.13), channel_id=1, source_target_pairs={{1,0},{2,1},{3,2},{4,3},{5,4},{6,5},{7,6},{9,8},{10,9},{11,10},{12... | collective-permute-start | bytes 36872 | tf_op jit(solution)/shard_map/ppermute | solution.py:13
  98.4 12.6 %collective-permute-start.8 = (f32[1,24,128]{2,1,0:T(8,128)S(1)}, f32[1,24,128]{2,1,0:T(8,128)S(1)}, u32[]{:S(2)}, u32[]{:S(2)}) collective-permute-start(f32[1,24,128]{2,1,0:T(8,128)S(1)} %get-tuple-element.20), channel_id=1, source_target_pairs={{0,8},{8,16},{16,24},{1,9},{9,17},{17,25},{2,10},{10,18},{18,26},{... | collective-permute-start | bytes 36872 | tf_op jit(solution)/shard_map/ppermute | solution.py:13
  100.3 15.5 %collective-permute-start.9 = (f32[1,24,128]{2,1,0:T(8,128)S(1)}, f32[1,24,128]{2,1,0:T(8,128)S(1)}, u32[]{:S(2)}, u32[]{:S(2)}) collective-permute-start(f32[1,24,128]{2,1,0:T(8,128)S(1)} %get-tuple-element.19), channel_id=1, source_target_pairs={{8,0},{16,8},{24,16},{9,1},{17,9},{25,17},{10,2},{18,10},{26,18},{... | collective-permute-start | bytes 36872 | tf_op jit(solution)/shard_map/ppermute | solution.py:13
  105.2 14.6 %collective-permute-start.10 = (f32[1,24,128]{2,1,0:T(8,128)S(1)}, f32[1,24,128]{2,1,0:T(8,128)S(1)}, u32[]{:S(2)}, u32[]{:S(2)}) collective-permute-start(f32[1,24,128]{2,1,0:T(8,128)S(1)} %get-tuple-element.18), channel_id=1, source_target_pairs={{0,1},{1,2},{2,3},{3,4},{4,5},{5,6},{6,7},{8,9},{9,10},{10,11},{11... | collective-permute-start | bytes 36872 | tf_op jit(solution)/shard_map/ppermute | solution.py:13
  107.7 13.7 %collective-permute-start.11 = (f32[1,24,128]{2,1,0:T(8,128)S(1)}, f32[1,24,128]{2,1,0:T(8,128)S(1)}, u32[]{:S(2)}, u32[]{:S(2)}) collective-permute-start(f32[1,24,128]{2,1,0:T(8,128)S(1)} %get-tuple-element.17), channel_id=1, source_target_pairs={{1,0},{2,1},{3,2},{4,3},{5,4},{6,5},{7,6},{9,8},{10,9},{11,10},{12... | collective-permute-start | bytes 36872 | tf_op jit(solution)/shard_map/ppermute | solution.py:13
  109.0 21.6 %collective-permute-start.4 = (bf16[1,128,3072]{1,2,0:T(8,128)(2,1)S(1)}, bf16[1,128,3072]{1,2,0:T(8,128)(2,1)S(1)}, u32[]{:S(2)}, u32[]{:S(2)}) collective-permute-start(bf16[1,128,3072]{1,2,0:T(8,128)(2,1)S(1)} %bitcast.153), channel_id=1, source_target_pairs={{0,8},{8,16},{16,24},{1,9},{9,17},{17,25},{2,10},{10,18},{18,26},{... | collective-permute-start | bytes 2359304 | tf_op jit(solution)/shard_map/ppermute | solution.py:13
  111.0 32.8 %collective-permute-start.5 = (bf16[1,128,3072]{1,2,0:T(8,128)(2,1)S(1)}, bf16[1,128,3072]{1,2,0:T(8,128)(2,1)S(1)}, u32[]{:S(2)}, u32[]{:S(2)}) collective-permute-start(bf16[1,128,3072]{1,2,0:T(8,128)(2,1)S(1)} %bitcast.152), channel_id=1, source_target_pairs={{8,0},{16,8},{24,16},{9,1},{17,9},{25,17},{10,2},{18,10},{26,18},{... | collective-permute-start | bytes 2359304 | tf_op jit(solution)/shard_map/ppermute | solution.py:13
  115.8 28.1 %collective-permute-start.6 = (bf16[1,128,3072]{1,2,0:T(8,128)(2,1)S(1)}, bf16[1,128,3072]{1,2,0:T(8,128)(2,1)S(1)}, u32[]{:S(2)}, u32[]{:S(2)}) collective-permute-start(bf16[1,128,3072]{1,2,0:T(8,128)(2,1)S(1)} %bitcast.151), channel_id=1, source_target_pairs={{0,1},{1,2},{2,3},{3,4},{4,5},{5,6},{6,7},{8,9},{9,10},{10,11},{11... | collective-permute-start | bytes 2359304 | tf_op jit(solution)/shard_map/ppermute | solution.py:13
  119.8 24.3 %collective-permute-start.7 = (bf16[1,128,3072]{1,2,0:T(8,128)(2,1)S(1)}, bf16[1,128,3072]{1,2,0:T(8,128)(2,1)S(1)}, u32[]{:S(2)}, u32[]{:S(2)}) collective-permute-start(bf16[1,128,3072]{1,2,0:T(8,128)(2,1)S(1)} %bitcast.150), channel_id=1, source_target_pairs={{1,0},{2,1},{3,2},{4,3},{5,4},{6,5},{7,6},{9,8},{10,9},{11,10},{12... | collective-permute-start | bytes 2359304 | tf_op jit(solution)/shard_map/ppermute | solution.py:13
  145.3 3.2 copy-start.2
  145.3 3.5 copy-start.5
  383.2 5.1 copy-start.4
  383.2 143.8 %all-to-all-start.1 = ((bf16[8,128,3072]{2,1,0:T(8,128)(2,1)}), bf16[8,128,3072]{2,1,0:T(8,128)(2,1)}, u32[]{:S(2)}, u32[]{:S(2)}) async-start(bf16[8,128,3072]{2,1,0:T(8,128)(2,1)} %bitcast.143), calls=%async_computation.1 | async-start | bytes 12582912 | tf_op jit(solution)/shard_map/all_to_all | solution.py:193
  540.0 12.8 %copy-start.1 = (bf16[128,3072]{1,0:T(8,128)(2,1)S(1)}, bf16[128,3072]{1,0:T(8,128)(2,1)}, u32[]{:S(2)}) copy-start(bf16[128,3072]{1,0:T(8,128)(2,1)} %param.12) | copy-start | bytes 2359300
where the time goes:
time: 559 us; the launch traced here: 553 us
  waiting for transfers between devices  191 us (34%)
  blocking collectives  147 us (26%)
  local copies, waits for them, and re-layouts  98.1 us (18%)
  starting transfers between devices  66 us (12%)
  matrix products  27.2 us (5%)
  other arithmetic  23.1 us (4%)
    all_to_all x1, blocking collectives, local(): lax.all_to_all(padded_out, 'row', split_axis=0, concat_axis=0, tiled=True)  147 us
    all_to_all x1, waiting for transfers between devices, local(): lax.all_to_all(result.reshape(arrived.shape), 'row', split_axis=0, concat...  138 us
    scatter x1, local copies, waits for them, and re-layouts, local(): outgoing = jnp.zeros((expert_count, capacity, features), jnp.bfloat16).at...  56.3 us
    ppermute x12, starting transfers between devices, shifted(): lax.ppermute(value, axis, [(source, source + steps) for source in range(i...  50.1 us
    ppermute x12, waiting for transfers between devices, shifted(): lax.ppermute(value, axis, [(source, source + steps) for source in range(i...  22.2 us
    dot_general x1, matrix products, half_expert(): jnp.dot(inner, w_down[0], preferred_element_type=jnp.float32)  19.4 us
    ppermute x2, waiting for transfers between devices, with_halo(): lax.ppermute(lax.slice_in_dim(block, block.shape[dim] - width, None, axis...  16.5 us
    ppermute x2, waiting for transfers between devices, with_halo(): lax.ppermute(lax.slice_in_dim(block, 0, width, axis=dim), axis, backward)  13.8 us
  transfers between devices with their start and end apart: 17, of which 5 were waited for; matrix products, arithmetic and copies ran while one was open for 2% of the time, Pallas kernels for 0%

commit v1 on v0

--- a/solution.py
+++ b/solution.py
@@ -1,6 +1,10 @@
+import functools
+
 import jax
 import jax.numpy as jnp
 from jax import lax
+from jax.experimental import pallas as pl
+from jax.experimental.pallas import tpu as pltpu
 from jax.sharding import PartitionSpec as P
 
 HEADS = 24
@@ -82,7 +86,7 @@
     return jnp.dot(inner, w_down[0], preferred_element_type=jnp.float32).astype(jnp.bfloat16)
 
 
-def local(
+def plain(
     layer_input, queries, key_input, values, key_tiles, expert_ids, norm_gain, router, w_up, w_down
 ):
     head_count = HEADS
@@ -199,6 +203,406 @@
     return (hidden_state + jnp.sum(gates[:, :, None] * picked, axis=1)).astype(jnp.bfloat16)
 
 
+HALO_PARTS = 4
+SUM_PARTS = 4
+MESH = pl.DeviceIdType.MESH
+
+
+def fused_kernel(
+    frames, rows, heads,
+    li, q, k, v, bias, gain, router, sel, wup_hbm, wdn_hbm,
+    out,
+    kb, vb, hid, g, p, sib, fd, fu, hmid, wup, wdn,
+    wsem, hsend, hrecv, agu, agd, ags, agr, pss, psr, ups, dns, upr, dnr,
+):
+    chips = rows // 2
+    features = q.shape[1]
+    f = lax.axis_index("frame")
+    r = lax.axis_index("row")
+    z = r // 2
+    c = r % 2
+    sibling = {"row": 2 * z + 1 - c}
+    above = {"row": r + 2}
+    below = {"row": r - 2}
+    has_above = z < chips - 1
+    has_below = z > 0
+    sides = (
+        (f > 0, {"frame": f - 1}, 1),
+        (f < frames - 1, {"frame": f + 1}, 0),
+        (r > 0, {"row": r - 1}, 3),
+        (r < rows - 1, {"row": r + 1}, 2),
+    )
+
+    load_up = pltpu.make_async_copy(wup_hbm.at[0], wup, wsem.at[0])
+    load_dn = pltpu.make_async_copy(wdn_hbm.at[0], wdn, wsem.at[1])
+    load_up.start()
+    load_dn.start()
+
+    barrier = pltpu.get_barrier_semaphore()
+    partners = sides + ((has_below, below, 0), (has_above, above, 0))
+    for there, who, _ in partners:
+        @pl.when(there)
+        def _():
+            pl.semaphore_signal(barrier, inc=1, device_id=who, device_id_type=MESH)
+    peers = sum(jnp.where(there, 1, 0) for there, _, _ in partners)
+    pl.semaphore_wait(barrier, peers)
+
+    width = features // HALO_PARTS
+
+    def halo(side, part, which):
+        _, who, slot = sides[side]
+        cols = pl.ds(part * width, width)
+        src, dst = ((k, kb), (v, vb))[which]
+        return pltpu.make_async_remote_copy(
+            src_ref=src.at[:, cols],
+            dst_ref=dst.at[slot, :, cols],
+            send_sem=hsend.at[side, part, which],
+            recv_sem=hrecv.at[slot, part, which],
+            device_id=who,
+            device_id_type=MESH,
+        )
+
+    def halo_arrival(slot, part, which):
+        cols = pl.ds(part * width, width)
+        src, dst = ((k, kb), (v, vb))[which]
+        return pltpu.make_async_remote_copy(
+            src_ref=src.at[:, cols],
+            dst_ref=dst.at[slot, :, cols],
+            send_sem=hsend.at[slot, part, which],
+            recv_sem=hrecv.at[slot, part, which],
+            device_id=sides[slot][1],
+            device_id_type=MESH,
+        )
+
+    for part in range(HALO_PARTS):
+        for side in range(4):
+            @pl.when(sides[side][0])
+            def _():
+                halo(side, part, 0).start()
+                halo(side, part, 1).start()
+    for slot in range(4):
+        @pl.when(jnp.logical_not(sides[slot][0]))
+        def _():
+            kb[slot] = jnp.zeros(kb.shape[1:], kb.dtype)
+            vb[slot] = jnp.zeros(vb.shape[1:], vb.dtype)
+
+    scale = TILE ** -0.5
+    per_part = heads // HALO_PARTS
+    for part in range(HALO_PARTS):
+        for slot in range(4):
+            @pl.when(sides[slot][0])
+            def _():
+                halo_arrival(slot, part, 0).wait_recv()
+                halo_arrival(slot, part, 1).wait_recv()
+
+        def one_head(h):
+            cols = pl.ds(pl.multiple_of(h * TILE, TILE), TILE)
+            keys = jnp.concatenate([k[:, cols]] + [kb[s, :, cols] for s in range(4)], axis=0)
+            vals = jnp.concatenate([v[:, cols]] + [vb[s, :, cols] for s in range(4)], axis=0)
+            scores = lax.dot_general(
+                q[:, cols], keys, (((1,), (1,)), ((), ())), preferred_element_type=jnp.float32
+            ) * scale + bias[...]
+            peak = jnp.max(scores, axis=1, keepdims=True)
+            probs = jnp.exp(scores - peak)
+            total = jnp.sum(probs, axis=1, keepdims=True)
+            mixed = jnp.dot(probs.astype(jnp.bfloat16), vals, preferred_element_type=jnp.float32)
+            hid[:, cols] = li[:, cols].astype(jnp.float32) + mixed / total
+
+        step = 3 if per_part % 3 == 0 else 1
+
+        @pl.loop(0, per_part // step)
+        def _(i):
+            for j in range(step):
+                one_head(part * per_part + i * step + j)
+
+    square = jnp.zeros((TILE, TILE), jnp.float32)
+    for h in range(heads):
+        piece = hid[:, h * TILE:(h + 1) * TILE]
+        square = square + piece * piece
+    inverse = lax.rsqrt(jnp.sum(square, axis=1, keepdims=True) / features + 1e-06)
+    logits = jnp.zeros((TILE, TILE), jnp.float32)
+    for h in range(heads):
+        cols = slice(h * TILE, (h + 1) * TILE)
+        piece = (hid[:, cols] * inverse * gain[:, cols]).astype(jnp.bfloat16)
+        g[r, :, cols] = piece
+        logits = logits + jnp.dot(piece, router[cols, :], preferred_element_type=jnp.float32)
+    gates = jax.nn.sigmoid(logits) * sel[...]
+    high = gates.astype(jnp.bfloat16)
+    low = (gates - high.astype(jnp.float32)).astype(jnp.bfloat16)
+    lane = lax.broadcasted_iota(jnp.int32, (TILE, TILE), 1)
+    g[r, :, features:] = jnp.where(
+        lane < TILE // 2, high.astype(jnp.float32), low.astype(jnp.float32)
+    ).astype(jnp.bfloat16)
+
+    def send(src, dst, send_sem, recv_sem, who):
+        return pltpu.make_async_remote_copy(
+            src_ref=src, dst_ref=dst, send_sem=send_sem, recv_sem=recv_sem,
+            device_id=who, device_id_type=MESH,
+        )
+
+    def block_up(t):
+        b = 2 * t + c
+        return send(g.at[b], g.at[b], agu.at[t], agr.at[b], above)
+
+    def block_down(t):
+        b = 2 * t + c
+        return send(g.at[b], g.at[b], agd.at[t], agr.at[b], below)
+
+    def block_side(t):
+        b = 2 * t + c
+        return send(g.at[b], g.at[b], ags.at[t], agr.at[b], sibling)
+
+    def block_arrival(b):
+        return send(g.at[b], g.at[b], ags.at[0], agr.at[b], sibling)
+
+    def part_side(t):
+        return send(p.at[2 * t + 1 - c], sib.at[t], pss.at[t], psr.at[t], sibling)
+
+    height = TILE // SUM_PARTS
+
+    def sum_up(t, n):
+        piece = pl.ds(n * height, height)
+        return send(p.at[2 * t + c, piece], fd.at[t, piece], ups.at[t, n], upr.at[t, n], above)
+
+    def sum_down(t, n):
+        piece = pl.ds(n * height, height)
+        return send(p.at[2 * t + c, piece], fu.at[t, piece], dns.at[t, n], dnr.at[t, n], below)
+
+    def expert_pair(t):
+        pair = pl.ds(2 * t, 2)
+
+        @pl.loop(0, hmid.shape[1] // 256)
+        def _(n):
+            cols = pl.ds(pl.multiple_of(n * 256, 256), 256)
+            tokens = g[pair, :, :features].reshape(2 * TILE, features)
+            up = jnp.dot(tokens, wup[:, cols], preferred_element_type=jnp.float32)
+            hmid[:, cols] = jax.nn.gelu(up, approximate=True).astype(jnp.bfloat16)
+
+        gate_lanes = g[pair, :, features:].reshape(2 * TILE, TILE).astype(jnp.float32)
+        lanes = lax.broadcasted_iota(jnp.int32, (2 * TILE, TILE), 1)
+        mine = (lanes == z) | (lanes == z + TILE // 2)
+        gate = jnp.sum(jnp.where(mine, gate_lanes, 0.0), axis=1, keepdims=True)
+
+        @pl.loop(0, features // 256)
+        def _(n):
+            cols = pl.ds(pl.multiple_of(n * 256, 256), 256)
+            down = jnp.dot(hmid[...], wdn[:, cols], preferred_element_type=jnp.float32)
+            p[pair, :, cols] = (down * gate).astype(jnp.bfloat16).reshape(2, TILE, 256)
+
+        part_side(t).start()
+
+    def chain(s):
+        up_to = s
+        down_to = chips - 1 - s
+        goes_up = z < up_to
+        goes_down = z > down_to
+
+        @pl.when(goes_up)
+        def _():
+            part_side_arrival(up_to)
+
+        @pl.when(goes_down)
+        def _():
+            part_side_arrival(down_to)
+
+        for n in range(SUM_PARTS):
+            piece = pl.ds(n * height, height)
+
+            @pl.when(goes_up)
+            def _():
+                own = p[2 * up_to + c, piece].astype(jnp.float32) + sib[up_to, piece].astype(jnp.float32)
+                p[2 * up_to + c, piece] = own.astype(jnp.bfloat16)
+
+                @pl.when(has_below)
+                def _():
+                    sum_up(up_to, n).wait_recv()
+                    p[2 * up_to + c, piece] = (own + fd[up_to, piece].astype(jnp.float32)).astype(jnp.bfloat16)
+
+                sum_up(up_to, n).start()
+
+            @pl.when(goes_down)
+            def _():
+                own = p[2 * down_to + c, piece].astype(jnp.float32) + sib[down_to, piece].astype(jnp.float32)
+                p[2 * down_to + c, piece] = own.astype(jnp.bfloat16)
+
+                @pl.when(has_above)
+                def _():
+                    sum_down(down_to, n).wait_recv()
+                    p[2 * down_to + c, piece] = (own + fu[down_to, piece].astype(jnp.float32)).astype(jnp.bfloat16)
+
+                sum_down(down_to, n).start()
+
+    def part_side_arrival(t):
+        part_side(t).wait_recv()
+
+    block_side(z).start()
+
+    @pl.when(has_above)
+    def _():
+        block_up(z).start()
+
+    @pl.when(has_below)
+    def _():
+        block_down(z).start()
+
+    load_up.wait()
+    load_dn.wait()
+    block_arrival(2 * z + 1 - c).wait_recv()
+    expert_pair(z)
+    for s in range(1, chips):
+        @pl.when(z >= s)
+        def _():
+            t = z - s
+            block_arrival(2 * t + c).wait_recv()
+            block_side(t).start()
+
+            @pl.when(has_above)
+            def _():
+                block_up(t).start()
+
+        @pl.when(z + s < chips)
+        def _():
+            t = z + s
+            block_arrival(2 * t + c).wait_recv()
+            block_side(t).start()
+
+            @pl.when(has_below)
+            def _():
+                block_down(t).start()
+
+        @pl.when(z >= s)
+        def _():
+            t = z - s
+            block_arrival(2 * t + 1 - c).wait_recv()
+            expert_pair(t)
+
+        @pl.when(z + s < chips)
+        def _():
+            t = z + s
+            block_arrival(2 * t + 1 - c).wait_recv()
+            expert_pair(t)
+
+        if s >= 2:
+            chain(s - 1)
+    chain(chips - 1)
+
+    part_side_arrival(z)
+    for n in range(SUM_PARTS):
+        piece = pl.ds(n * height, height)
+        hid[piece] = hid[piece] + (
+            p[2 * z + c, piece].astype(jnp.float32) + sib[z, piece].astype(jnp.float32)
+        )
+
+        @pl.when(has_below)
+        def _():
+            sum_up(z, n).wait_recv()
+            hid[piece] = hid[piece] + fd[z, piece].astype(jnp.float32)
+
+        @pl.when(has_above)
+        def _():
+            sum_down(z, n).wait_recv()
+            hid[piece] = hid[piece] + fu[z, piece].astype(jnp.float32)
+
+        out[piece] = hid[piece].astype(jnp.bfloat16)
+
+    for part in range(HALO_PARTS):
+        for side in range(4):
+            @pl.when(sides[side][0])
+            def _():
+                halo(side, part, 0).wait_send()
+                halo(side, part, 1).wait_send()
+    for t in range(chips):
+        block_side(t).wait_send()
+        part_side(t).wait_send()
+
+        @pl.when((t <= z) & has_above)
+        def _():
+            block_up(t).wait_send()
+
+        @pl.when((t >= z) & has_below)
+        def _():
+            block_down(t).wait_send()
+
+        for n in range(SUM_PARTS):
+            @pl.when(z < t)
+            def _():
+                sum_up(t, n).wait_send()
+
+            @pl.when(z > t)
+            def _():
+                sum_down(t, n).wait_send()
+
+
+def local(
+    layer_input, queries, key_input, values, key_tiles, expert_ids, norm_gain, router, w_up, w_down
+):
+    frames = lax.axis_size("frame")
+    rows = lax.axis_size("row")
+    features = layer_input.shape[1]
+    experts = router.shape[1]
+    if rows > 8:
+        return plain(
+            layer_input, queries, key_input, values, key_tiles, expert_ids, norm_gain, router,
+            w_up, w_down,
+        )
+    f = lax.axis_index("frame")
+    r = lax.axis_index("row")
+    tile = f * rows + r
+    candidates = jnp.stack([tile, tile - rows, tile + rows, tile - 1, tile + 1])
+    inside = jnp.stack([r >= 0, f >= 1, f < frames - 1, r >= 1, r < rows - 1])
+    listed = inside & jnp.any(key_tiles[0][:, None] == candidates[None, :], axis=0)
+    bias = jnp.repeat(jnp.where(listed, 0.0, -1e30).astype(jnp.float32), TILE)[None, :]
+    half = TILE // 2
+    padded = jnp.pad(router, ((0, 0), (0, half - experts)))
+    padded = jnp.concatenate([padded, padded], axis=1)
+    lanes = jnp.arange(TILE, dtype=jnp.int32) % half
+    sel = jnp.any(expert_ids[:, :, None] == lanes[None, None, :], axis=1).astype(jnp.float32)
+    hidden = w_up.shape[2]
+    bf = jnp.bfloat16
+    chips = rows // 2
+    dma = pltpu.SemaphoreType.DMA
+    vmem = pl.BlockSpec(memory_space=pltpu.VMEM)
+    anywhere = pl.BlockSpec(memory_space=pl.ANY)
+    return pl.pallas_call(
+        functools.partial(fused_kernel, frames, rows, features // TILE),
+        out_shape=jax.ShapeDtypeStruct((TILE, features), bf),
+        in_specs=[vmem] * 8 + [anywhere] * 2,
+        out_specs=vmem,
+        scratch_shapes=[
+            pltpu.VMEM((4, TILE, features), bf),
+            pltpu.VMEM((4, TILE, features), bf),
+            pltpu.VMEM((TILE, features), jnp.float32),
+            pltpu.VMEM((rows, TILE, features + TILE), bf),
+            pltpu.VMEM((rows, TILE, features), bf),
+            pltpu.VMEM((chips, TILE, features), bf),
+            pltpu.VMEM((chips, TILE, features), bf),
+            pltpu.VMEM((chips, TILE, features), bf),
+            pltpu.VMEM((2 * TILE, hidden), bf),
+            pltpu.VMEM((features, hidden), bf),
+            pltpu.VMEM((hidden, features), bf),
+            dma((2,)),
+            dma((4, HALO_PARTS, 2)),
+            dma((4, HALO_PARTS, 2)),
+            dma((chips,)),
+            dma((chips,)),
+            dma((chips,)),
+            dma((rows,)),
+            dma((chips,)),
+            dma((chips,)),
+            dma((chips, SUM_PARTS)),
+            dma((chips, SUM_PARTS)),
+            dma((chips, SUM_PARTS)),
+            dma((chips, SUM_PARTS)),
+        ],
+        compiler_params=pltpu.CompilerParams(
+            collective_id=0, has_side_effects=True, vmem_limit_bytes=60 * 2**20
+        ),
+    )(
+        layer_input, queries, key_input, values, bias, norm_gain[None, :], padded, sel,
+        w_up, w_down,
+    )
+
+
 def solution(mesh):
     return jax.shard_map(
         local,

time: 559 us -> 220 us (0.39); the launches traced: 553 us -> 220 us
  Pallas kernels: 0 us -> 212 us
  waiting for transfers between devices: 191 us -> 0 us
  blocking collectives: 147 us -> 0 us
  local copies, waits for them, and re-layouts: 98.1 us -> 4.22 us
  starting transfers between devices: 66 us -> 0 us
  matrix products: 27.2 us -> 0 us
  other arithmetic: 23.1 us -> 3.47 us
    pallas_call x0 -> x1, Pallas kernels: none -> 212 us  [local(): pl.pallas_call(functools.partial(fused_kernel, frames, rows, features //...]
    all_to_all x1 -> x0, blocking collectives: 147 us -> none  [local(): lax.all_to_all(padded_out, 'row', split_axis=0, concat_axis=0, tiled=True)]
    all_to_all x1 -> x0, waiting for transfers between devices: 138 us -> none  [local(): lax.all_to_all(result.reshape(arrived.shape), 'row', split_axis=0, concat...]
    ppermute x16 -> x0, starting transfers between devices: 60.9 us -> none  [the longest x12 50.1 us: shifted(): lax.ppermute(value, axis, [(source, source + steps) for source in range(i...]
    scatter x1 -> x0, local copies, waits for them, and re-layouts: 56.3 us -> none  [local(): outgoing = jnp.zeros((expert_count, capacity, features), jnp.bfloat16).at...]
    ppermute x16 -> x0, waiting for transfers between devices: 52.5 us -> none  [the longest x12 22.2 us: shifted(): lax.ppermute(value, axis, [(source, source + steps) for source in range(i...]
    dot_general x4 -> x0, matrix products: 27.2 us -> none  [the longest x1 19.4 us: half_expert(): jnp.dot(inner, w_down[0], preferred_element_type=jnp.float32)]
    reduce_sum x7 -> x0, other arithmetic: 10.4 us -> none  [the longest x1 6.44 us: local(): jnp.sum(gates[:, :, None] * picked, axis=1)]
  transfers between devices with their start and end apart: 17 -> 0, of which waited for: 5 -> 0; matrix products, arithmetic and copies ran while one was open for 2% -> 0% of each run, Pallas kernels for 0% -> 0%
where the time goes in v1:
time: 220 us
  Pallas kernels  212 us (96%)
  local copies, waits for them, and re-layouts  4.22 us (2%)
  other arithmetic  3.47 us (2%)
    pallas_call x1, Pallas kernels, local(): pl.pallas_call(functools.partial(fused_kernel, frames, rows, features //...  212 us

profile of v1, /device:TPU:4, one launch (start us, length us, event | category | flops | bytes accessed | tf_op | source)
XLA Modules:
  0.0 220.0 jit_solution(507402813400179038)
XLA Ops:
  0.0 0.1 stack.41
  0.1 0.1 stack.47
  0.2 0.7 compare_reduce_fusion.1
  0.9 0.1 broadcast_bitcast_fusion
  1.0 0.6 copy.16
  1.6 0.8 compare_reduce_fusion
  2.4 0.6 convert_element_type.5.sel
  3.0 1.2 copy.13
  4.2 0.2 pad.4
  4.3 1.3 pad_maximum_fusion.router
  5.6 212.3 %shard_map.100 = bf16[128,3072]{1,0:T(8,128)(2,1)} custom-call(bf16[128,3072]{1,0:T(8,128)(2,1)} %li.1, bf16[128,3072]{1,0:T(8,128)(2,1)} %q.1, bf16[128,3072]{1,0:T(8,128)(2,1)} %k.1, bf16[128,3072]{1,0:T(8,128)(2,1)} %v.1, f32[1,640]{1,0:T(1,128)} %bitcast.19, f32[1,3072]{1,0:T(1,128)} %bitcast.18, bf16[3072,128]{1,0:T(8,128)(2,1)} %pad_maximum_fusion.router, ...), custom_call_target="tpu_custom_call" | custom-call | tf_op jit(solution)/shard_map/pallas_call | solution.py:566
  217.9 2.1 copy.18
  (2 shorter events, 0.0 us)

commit v2 on v1

--- a/solution.py
+++ b/solution.py
@@ -203,7 +203,7 @@
     return (hidden_state + jnp.sum(gates[:, :, None] * picked, axis=1)).astype(jnp.bfloat16)
 
 
-HALO_PARTS = 4
+HALO_PARTS = 6
 SUM_PARTS = 4
 MESH = pl.DeviceIdType.MESH
 
@@ -212,7 +212,7 @@
     frames, rows, heads,
     li, q, k, v, bias, gain, router, sel, wup_hbm, wdn_hbm,
     out,
-    kb, vb, hid, g, p, sib, fd, fu, hmid, wup, wdn,
+    kb, vb, hid, square, logits, g, p, sib, fd, fu, hmid, wup, wdn,
     wsem, hsend, hrecv, agu, agd, ags, agr, pss, psr, ups, dns, upr, dnr,
 ):
     chips = rows // 2
@@ -226,6 +226,8 @@
     below = {"row": r - 2}
     has_above = z < chips - 1
     has_below = z > 0
+    relayed = frames == 4
+    first, last = f == 0, f == frames - 1
     sides = (
         (f > 0, {"frame": f - 1}, 1),
         (f < frames - 1, {"frame": f + 1}, 0),
@@ -240,6 +242,12 @@
 
     barrier = pltpu.get_barrier_semaphore()
     partners = sides + ((has_below, below, 0), (has_above, above, 0))
+    if relayed:
+        partners += ((f >= 0, {"frame": lax.rem(f + 2, 4)}, 0),)
+    direct = [side[0] for side in sides]
+    if relayed:
+        direct[0] = direct[0] & (f != 2)
+        direct[1] = direct[1] & (f != 1)
     for there, who, _ in partners:
         @pl.when(there)
         def _():
@@ -274,9 +282,21 @@
             device_id_type=MESH,
         )
 
+    def relay(slot, part, which):
+        cols = pl.ds(part * width, width)
+        buffer = (kb, vb)[which]
+        return pltpu.make_async_remote_copy(
+            src_ref=buffer.at[1 - slot, :, cols],
+            dst_ref=buffer.at[slot, :, cols],
+            send_sem=hsend.at[slot, part, which],
+            recv_sem=hrecv.at[slot, part, which],
+            device_id={"frame": lax.rem(f + 2, 4)},
+            device_id_type=MESH,
+        )
+
     for part in range(HALO_PARTS):
         for side in range(4):
-            @pl.when(sides[side][0])
+            @pl.when(direct[side])
             def _():
                 halo(side, part, 0).start()
                 halo(side, part, 1).start()
@@ -286,6 +306,72 @@
             kb[slot] = jnp.zeros(kb.shape[1:], kb.dtype)
             vb[slot] = jnp.zeros(vb.shape[1:], vb.dtype)
 
+    def send(src, dst, send_sem, recv_sem, who):
+        return pltpu.make_async_remote_copy(
+            src_ref=src, dst_ref=dst, send_sem=send_sem, recv_sem=recv_sem,
+            device_id=who, device_id_type=MESH,
+        )
+
+    def stretch(b, part):
+        if part == HALO_PARTS:
+            return g.at[b, :, pl.ds(features, TILE)]
+        return g.at[b, :, pl.ds(part * width, width)]
+
+    def block_up(t, part):
+        b = 2 * t + c
+        return send(stretch(b, part), stretch(b, part), agu.at[t, part], agr.at[b, part], above)
+
+    def block_down(t, part):
+        b = 2 * t + c
+        return send(stretch(b, part), stretch(b, part), agd.at[t, part], agr.at[b, part], below)
+
+    def block_side(t, part):
+        b = 2 * t + c
+        return send(stretch(b, part), stretch(b, part), ags.at[t, part], agr.at[b, part], sibling)
+
+    def block_arrival(b, part):
+        return send(stretch(b, part), stretch(b, part), ags.at[0, part], agr.at[b, part], sibling)
+
+    def gather(stage):
+        if stage <= HALO_PARTS:
+            @pl.when(has_above)
+            def _():
+                block_up(z, stage).start()
+
+            @pl.when(has_below)
+            def _():
+                block_down(z, stage).start()
+
+            block_side(z, stage).start()
+        for d in range(1, chips):
+            part = stage - d
+            if part < 0 or part > HALO_PARTS:
+                continue
+
+            @pl.when(z >= d)
+            def _():
+                t = z - d
+                block_arrival(2 * t + c, part).wait_recv()
+
+                @pl.when(has_above)
+                def _():
+                    block_up(t, part).start()
+
+                block_side(t, part).start()
+
+            @pl.when(z + d < chips)
+            def _():
+                t = z + d
+                block_arrival(2 * t + c, part).wait_recv()
+
+                @pl.when(has_below)
+                def _():
+                    block_down(t, part).start()
+
+                block_side(t, part).start()
+
+    square[...] = jnp.zeros_like(square)
+    logits[...] = jnp.zeros_like(logits)
     scale = TILE ** -0.5
     per_part = heads // HALO_PARTS
     for part in range(HALO_PARTS):
@@ -294,6 +380,12 @@
             def _():
                 halo_arrival(slot, part, 0).wait_recv()
                 halo_arrival(slot, part, 1).wait_recv()
+
+            if relayed and slot < 2:
+                @pl.when(last if slot == 0 else first)
+                def _():
+                    relay(1 - slot, part, 0).start()
+                    relay(1 - slot, part, 1).start()
 
         def one_head(h):
             cols = pl.ds(pl.multiple_of(h * TILE, TILE), TILE)
@@ -306,54 +398,36 @@
             probs = jnp.exp(scores - peak)
             total = jnp.sum(probs, axis=1, keepdims=True)
             mixed = jnp.dot(probs.astype(jnp.bfloat16), vals, preferred_element_type=jnp.float32)
-            hid[:, cols] = li[:, cols].astype(jnp.float32) + mixed / total
-
-        step = 3 if per_part % 3 == 0 else 1
+            state = li[:, cols].astype(jnp.float32) + mixed / total
+            hid[:, cols] = state
+            square[...] = square[...] + state * state
+            token = (state * gain[:, cols]).astype(jnp.bfloat16)
+            g[r, :, cols] = token
+            logits[...] = logits[...] + jnp.dot(
+                token, router[cols, :], preferred_element_type=jnp.float32
+            )
+
+        step = 2 if per_part % 2 == 0 else 1
 
         @pl.loop(0, per_part // step)
         def _(i):
             for j in range(step):
                 one_head(part * per_part + i * step + j)
 
-    square = jnp.zeros((TILE, TILE), jnp.float32)
-    for h in range(heads):
-        piece = hid[:, h * TILE:(h + 1) * TILE]
-        square = square + piece * piece
-    inverse = lax.rsqrt(jnp.sum(square, axis=1, keepdims=True) / features + 1e-06)
-    logits = jnp.zeros((TILE, TILE), jnp.float32)
-    for h in range(heads):
-        cols = slice(h * TILE, (h + 1) * TILE)
-        piece = (hid[:, cols] * inverse * gain[:, cols]).astype(jnp.bfloat16)
-        g[r, :, cols] = piece
-        logits = logits + jnp.dot(piece, router[cols, :], preferred_element_type=jnp.float32)
-    gates = jax.nn.sigmoid(logits) * sel[...]
+        gather(part)
+
+    inverse = lax.rsqrt(jnp.sum(square[...], axis=1, keepdims=True) / features + 1e-06)
+    gates = jax.nn.sigmoid(logits[...] * inverse) * sel[...]
+    lane = lax.broadcasted_iota(jnp.int32, (TILE, TILE), 1)
+    gates = jnp.where((lane == TILE // 4) | (lane == 3 * TILE // 4), inverse, gates)
     high = gates.astype(jnp.bfloat16)
     low = (gates - high.astype(jnp.float32)).astype(jnp.bfloat16)
-    lane = lax.broadcasted_iota(jnp.int32, (TILE, TILE), 1)
     g[r, :, features:] = jnp.where(
         lane < TILE // 2, high.astype(jnp.float32), low.astype(jnp.float32)
     ).astype(jnp.bfloat16)
 
-    def send(src, dst, send_sem, recv_sem, who):
-        return pltpu.make_async_remote_copy(
-            src_ref=src, dst_ref=dst, send_sem=send_sem, recv_sem=recv_sem,
-            device_id=who, device_id_type=MESH,
-        )
-
-    def block_up(t):
-        b = 2 * t + c
-        return send(g.at[b], g.at[b], agu.at[t], agr.at[b], above)
-
-    def block_down(t):
-        b = 2 * t + c
-        return send(g.at[b], g.at[b], agd.at[t], agr.at[b], below)
-
-    def block_side(t):
-        b = 2 * t + c
-        return send(g.at[b], g.at[b], ags.at[t], agr.at[b], sibling)
-
-    def block_arrival(b):
-        return send(g.at[b], g.at[b], ags.at[0], agr.at[b], sibling)
+    for stage in range(HALO_PARTS, HALO_PARTS + chips):
+        gather(stage)
 
     def part_side(t):
         return send(p.at[2 * t + 1 - c], sib.at[t], pss.at[t], psr.at[t], sibling)
@@ -370,18 +444,19 @@
 
     def expert_pair(t):
         pair = pl.ds(2 * t, 2)
+        tail = g[pair, :, features:].reshape(2 * TILE, TILE).astype(jnp.float32)
+        lanes = lax.broadcasted_iota(jnp.int32, (2 * TILE, TILE), 1)
+        mine = (lanes == z) | (lanes == z + TILE // 2)
+        gate = jnp.sum(jnp.where(mine, tail, 0.0), axis=1, keepdims=True)
+        norms = (lanes == TILE // 4) | (lanes == 3 * TILE // 4)
+        inverse = jnp.sum(jnp.where(norms, tail, 0.0), axis=1, keepdims=True)
 
         @pl.loop(0, hmid.shape[1] // 256)
         def _(n):
             cols = pl.ds(pl.multiple_of(n * 256, 256), 256)
             tokens = g[pair, :, :features].reshape(2 * TILE, features)
             up = jnp.dot(tokens, wup[:, cols], preferred_element_type=jnp.float32)
-            hmid[:, cols] = jax.nn.gelu(up, approximate=True).astype(jnp.bfloat16)
-
-        gate_lanes = g[pair, :, features:].reshape(2 * TILE, TILE).astype(jnp.float32)
-        lanes = lax.broadcasted_iota(jnp.int32, (2 * TILE, TILE), 1)
-        mine = (lanes == z) | (lanes == z + TILE // 2)
-        gate = jnp.sum(jnp.where(mine, gate_lanes, 0.0), axis=1, keepdims=True)
+            hmid[:, cols] = jax.nn.gelu(up * inverse, approximate=True).astype(jnp.bfloat16)
 
         @pl.loop(0, features // 256)
         def _(n):
@@ -391,100 +466,67 @@
 
         part_side(t).start()
 
-    def chain(s):
-        up_to = s
-        down_to = chips - 1 - s
-        goes_up = z < up_to
-        goes_down = z > down_to
-
-        @pl.when(goes_up)
-        def _():
-            part_side_arrival(up_to)
-
-        @pl.when(goes_down)
-        def _():
-            part_side_arrival(down_to)
-
+    def part_side_arrival(t):
+        part_side(t).wait_recv()
+
+    def pass_up(t, head):
+        part_side_arrival(t)
         for n in range(SUM_PARTS):
             piece = pl.ds(n * height, height)
-
-            @pl.when(goes_up)
-            def _():
-                own = p[2 * up_to + c, piece].astype(jnp.float32) + sib[up_to, piece].astype(jnp.float32)
-                p[2 * up_to + c, piece] = own.astype(jnp.bfloat16)
-
-                @pl.when(has_below)
-                def _():
-                    sum_up(up_to, n).wait_recv()
-                    p[2 * up_to + c, piece] = (own + fd[up_to, piece].astype(jnp.float32)).astype(jnp.bfloat16)
-
-                sum_up(up_to, n).start()
-
-            @pl.when(goes_down)
-            def _():
-                own = p[2 * down_to + c, piece].astype(jnp.float32) + sib[down_to, piece].astype(jnp.float32)
-                p[2 * down_to + c, piece] = own.astype(jnp.bfloat16)
-
-                @pl.when(has_above)
-                def _():
-                    sum_down(down_to, n).wait_recv()
-                    p[2 * down_to + c, piece] = (own + fu[down_to, piece].astype(jnp.float32)).astype(jnp.bfloat16)
-
-                sum_down(down_to, n).start()
-
-    def part_side_arrival(t):
-        part_side(t).wait_recv()
-
-    block_side(z).start()
-
-    @pl.when(has_above)
-    def _():
-        block_up(z).start()
-
-    @pl.when(has_below)
-    def _():
-        block_down(z).start()
+            total = p[2 * t + c, piece].astype(jnp.float32) + sib[t, piece].astype(jnp.float32)
+            if not head:
+                sum_up(t, n).wait_recv()
+                total = total + fd[t, piece].astype(jnp.float32)
+            p[2 * t + c, piece] = total.astype(jnp.bfloat16)
+            sum_up(t, n).start()
+
+    def pass_down(t, head):
+        part_side_arrival(t)
+        for n in range(SUM_PARTS):
+            piece = pl.ds(n * height, height)
+            total = p[2 * t + c, piece].astype(jnp.float32) + sib[t, piece].astype(jnp.float32)
+            if not head:
+                sum_down(t, n).wait_recv()
+                total = total + fu[t, piece].astype(jnp.float32)
+            p[2 * t + c, piece] = total.astype(jnp.bfloat16)
+            sum_down(t, n).start()
 
     load_up.wait()
     load_dn.wait()
-    block_arrival(2 * z + 1 - c).wait_recv()
+    for t in range(chips):
+        for part in range(HALO_PARTS + 1):
+            block_arrival(2 * t + 1 - c, part).wait_recv()
+
+    for s in range(chips - 1, 0, -1):
+        far = chips - 1 - s
+
+        @pl.when(z < s)
+        def _():
+            expert_pair(s)
+
+        @pl.when(z == 0)
+        def _():
+            pass_up(s, True)
+
+        @pl.when(z > far)
+        def _():
+            expert_pair(far)
+
+        @pl.when(z == chips - 1)
+        def _():
+            pass_down(far, True)
+
     expert_pair(z)
-    for s in range(1, chips):
-        @pl.when(z >= s)
-        def _():
-            t = z - s
-            block_arrival(2 * t + c).wait_recv()
-            block_side(t).start()
-
-            @pl.when(has_above)
-            def _():
-                block_up(t).start()
-
-        @pl.when(z + s < chips)
-        def _():
-            t = z + s
-            block_arrival(2 * t + c).wait_recv()
-            block_side(t).start()
-
-            @pl.when(has_below)
-            def _():
-                block_down(t).start()
-
-        @pl.when(z >= s)
-        def _():
-            t = z - s
-            block_arrival(2 * t + 1 - c).wait_recv()
-            expert_pair(t)
-
-        @pl.when(z + s < chips)
-        def _():
-            t = z + s
-            block_arrival(2 * t + 1 - c).wait_recv()
-            expert_pair(t)
-
-        if s >= 2:
-            chain(s - 1)
-    chain(chips - 1)
+    for s in range(chips - 1, 0, -1):
+        far = chips - 1 - s
+
+        @pl.when((z < s) & has_below)
+        def _():
+            pass_up(s, False)
+
+        @pl.when((z > far) & has_above)
+        def _():
+            pass_down(far, False)
 
     part_side_arrival(z)
     for n in range(SUM_PARTS):
@@ -507,21 +549,33 @@
 
     for part in range(HALO_PARTS):
         for side in range(4):
-            @pl.when(sides[side][0])
+            @pl.when(direct[side])
             def _():
                 halo(side, part, 0).wait_send()
                 halo(side, part, 1).wait_send()
+
+        if relayed:
+            @pl.when(first)
+            def _():
+                relay(0, part, 0).wait_send()
+                relay(0, part, 1).wait_send()
+
+            @pl.when(last)
+            def _():
+                relay(1, part, 0).wait_send()
+                relay(1, part, 1).wait_send()
     for t in range(chips):
-        block_side(t).wait_send()
         part_side(t).wait_send()
-
-        @pl.when((t <= z) & has_above)
-        def _():
-            block_up(t).wait_send()
-
-        @pl.when((t >= z) & has_below)
-        def _():
-            block_down(t).wait_send()
+        for part in range(HALO_PARTS + 1):
+            block_side(t, part).wait_send()
+
+            @pl.when((t <= z) & has_above)
+            def _():
+                block_up(t, part).wait_send()
+
+            @pl.when((t >= z) & has_below)
+            def _():
+                block_down(t, part).wait_send()
 
         for n in range(SUM_PARTS):
             @pl.when(z < t)
@@ -572,6 +626,8 @@
             pltpu.VMEM((4, TILE, features), bf),
             pltpu.VMEM((4, TILE, features), bf),
             pltpu.VMEM((TILE, features), jnp.float32),
+            pltpu.VMEM((TILE, TILE), jnp.float32),
+            pltpu.VMEM((TILE, TILE), jnp.float32),
             pltpu.VMEM((rows, TILE, features + TILE), bf),
             pltpu.VMEM((rows, TILE, features), bf),
             pltpu.VMEM((chips, TILE, features), bf),
@@ -583,10 +639,10 @@
             dma((2,)),
             dma((4, HALO_PARTS, 2)),
             dma((4, HALO_PARTS, 2)),
-            dma((chips,)),
-            dma((chips,)),
-            dma((chips,)),
-            dma((rows,)),
+            dma((chips, HALO_PARTS + 1)),
+            dma((chips, HALO_PARTS + 1)),
+            dma((chips, HALO_PARTS + 1)),
+            dma((rows, HALO_PARTS + 1)),
             dma((chips,)),
             dma((chips,)),
             dma((chips, SUM_PARTS)),

time: 220 us -> 163 us (0.74)
  the two profiles are of different devices: /device:TPU:4 before, /device:TPU:20 now
where the time goes in v2:
time: 163 us; the launch traced here: 162 us
  Pallas kernels  155 us (95%)
  local copies, waits for them, and re-layouts  4.22 us (3%)
  other arithmetic  3.47 us (2%)
    pallas_call x1, Pallas kernels, local(): pl.pallas_call(functools.partial(fused_kernel, frames, rows, features //...  155 us
    unnamed x4, local copies, waits for them, and re-layouts  3.88 us

profile of v2, /device:TPU:20, one launch (start us, length us, event | category | flops | bytes accessed | tf_op | source)
XLA Modules:
  0.0 162.3 jit_solution(16962646173689113485)
XLA Ops:
  0.0 0.1 stack.41
  0.1 0.1 stack.47
  0.2 0.7 compare_reduce_fusion.1
  0.9 0.1 broadcast_bitcast_fusion
  1.0 0.6 copy.16
  1.6 0.8 compare_reduce_fusion
  2.4 0.6 convert_element_type.5.sel
  3.0 1.2 copy.13
  4.2 0.2 pad.4
  4.3 1.3 pad_maximum_fusion.router
  5.6 154.6 %shard_map.100 = bf16[128,3072]{1,0:T(8,128)(2,1)} custom-call(bf16[128,3072]{1,0:T(8,128)(2,1)} %li.1, bf16[128,3072]{1,0:T(8,128)(2,1)} %q.1, bf16[128,3072]{1,0:T(8,128)(2,1)} %k.1, bf16[128,3072]{1,0:T(8,128)(2,1)} %v.1, f32[1,640]{1,0:T(1,128)} %bitcast.19, f32[1,3072]{1,0:T(1,128)} %bitcast.18, bf16[3072,128]{1,0:T(8,128)(2,1)} %pad_maximum_fusion.router, ...), custom_call_target="tpu_custom_call" | custom-call | tf_op jit(solution)/shard_map/pallas_call | solution.py:620
  160.2 2.1 %copy.18 = bf16[128,3072]{1,0:T(8,128)(2,1)} copy(bf16[128,3072]{1,0:T(8,128)(2,1)} %shard_map.100) | data formatting | bytes 1572864
  (2 shorter events, 0.0 us)

commit v3 on v2

--- a/solution.py
+++ b/solution.py
@@ -205,6 +205,7 @@
 
 HALO_PARTS = 6
 SUM_PARTS = 4
+LAG = 2
 MESH = pl.DeviceIdType.MESH
 
 
@@ -332,43 +333,42 @@
     def block_arrival(b, part):
         return send(stretch(b, part), stretch(b, part), ags.at[0, part], agr.at[b, part], sibling)
 
-    def gather(stage):
-        if stage <= HALO_PARTS:
+    def send_own(part):
+        @pl.when(has_above)
+        def _():
+            block_up(z, part).start()
+
+        @pl.when(has_below)
+        def _():
+            block_down(z, part).start()
+
+        block_side(z, part).start()
+
+    def forward(d, part):
+        if d >= chips:
+            return
+
+        @pl.when(z >= d)
+        def _():
+            t = z - d
+            block_arrival(2 * t + c, part).wait_recv()
+
             @pl.when(has_above)
             def _():
-                block_up(z, stage).start()
+                block_up(t, part).start()
+
+            block_side(t, part).start()
+
+        @pl.when(z + d < chips)
+        def _():
+            t = z + d
+            block_arrival(2 * t + c, part).wait_recv()
 
             @pl.when(has_below)
             def _():
-                block_down(z, stage).start()
-
-            block_side(z, stage).start()
-        for d in range(1, chips):
-            part = stage - d
-            if part < 0 or part > HALO_PARTS:
-                continue
-
-            @pl.when(z >= d)
-            def _():
-                t = z - d
-                block_arrival(2 * t + c, part).wait_recv()
-
-                @pl.when(has_above)
-                def _():
-                    block_up(t, part).start()
-
-                block_side(t, part).start()
-
-            @pl.when(z + d < chips)
-            def _():
-                t = z + d
-                block_arrival(2 * t + c, part).wait_recv()
-
-                @pl.when(has_below)
-                def _():
-                    block_down(t, part).start()
-
-                block_side(t, part).start()
+                block_down(t, part).start()
+
+            block_side(t, part).start()
 
     square[...] = jnp.zeros_like(square)
     logits[...] = jnp.zeros_like(logits)
@@ -414,7 +414,9 @@
             for j in range(step):
                 one_head(part * per_part + i * step + j)
 
-        gather(part)
+        send_own(part)
+        if part >= LAG:
+            forward(1, part - LAG)
 
     inverse = lax.rsqrt(jnp.sum(square[...], axis=1, keepdims=True) / features + 1e-06)
     gates = jax.nn.sigmoid(logits[...] * inverse) * sel[...]
@@ -426,8 +428,11 @@
         lane < TILE // 2, high.astype(jnp.float32), low.astype(jnp.float32)
     ).astype(jnp.bfloat16)
 
-    for stage in range(HALO_PARTS, HALO_PARTS + chips):
-        gather(stage)
+    send_own(HALO_PARTS)
+    for part in range(HALO_PARTS - LAG, HALO_PARTS + 1):
+        forward(1, part)
+    for part in range(HALO_PARTS - LAG):
+        forward(2, part)
 
     def part_side(t):
         return send(p.at[2 * t + 1 - c], sib.at[t], pss.at[t], psr.at[t], sibling)
@@ -469,64 +474,80 @@
     def part_side_arrival(t):
         part_side(t).wait_recv()
 
-    def pass_up(t, head):
-        part_side_arrival(t)
-        for n in range(SUM_PARTS):
-            piece = pl.ds(n * height, height)
-            total = p[2 * t + c, piece].astype(jnp.float32) + sib[t, piece].astype(jnp.float32)
-            if not head:
-                sum_up(t, n).wait_recv()
-                total = total + fd[t, piece].astype(jnp.float32)
-            p[2 * t + c, piece] = total.astype(jnp.bfloat16)
-            sum_up(t, n).start()
-
-    def pass_down(t, head):
-        part_side_arrival(t)
-        for n in range(SUM_PARTS):
-            piece = pl.ds(n * height, height)
-            total = p[2 * t + c, piece].astype(jnp.float32) + sib[t, piece].astype(jnp.float32)
-            if not head:
-                sum_down(t, n).wait_recv()
-                total = total + fu[t, piece].astype(jnp.float32)
-            p[2 * t + c, piece] = total.astype(jnp.bfloat16)
-            sum_down(t, n).start()
+    def pass_up(t, n, head):
+        piece = pl.ds(n * height, height)
+        total = p[2 * t + c, piece].astype(jnp.float32) + sib[t, piece].astype(jnp.float32)
+        if not head:
+            sum_up(t, n).wait_recv()
+            total = total + fd[t, piece].astype(jnp.float32)
+        p[2 * t + c, piece] = total.astype(jnp.bfloat16)
+        sum_up(t, n).start()
+
+    def pass_down(t, n, head):
+        piece = pl.ds(n * height, height)
+        total = p[2 * t + c, piece].astype(jnp.float32) + sib[t, piece].astype(jnp.float32)
+        if not head:
+            sum_down(t, n).wait_recv()
+            total = total + fu[t, piece].astype(jnp.float32)
+        p[2 * t + c, piece] = total.astype(jnp.bfloat16)
+        sum_down(t, n).start()
+
+    def experts_of(t):
+        for part in range(HALO_PARTS + 1):
+            block_arrival(2 * t + 1 - c, part).wait_recv()
+        expert_pair(t)
 
     load_up.wait()
     load_dn.wait()
-    for t in range(chips):
-        for part in range(HALO_PARTS + 1):
-            block_arrival(2 * t + 1 - c, part).wait_recv()
-
-    for s in range(chips - 1, 0, -1):
+    experts_of(z)
+    for part in range(HALO_PARTS - LAG, HALO_PARTS + 1):
+        forward(2, part)
+    for d in range(1, chips):
+        @pl.when(z >= d)
+        def _():
+            experts_of(z - d)
+
+            @pl.when(z == chips - 1)
+            def _():
+                part_side_arrival(chips - 1 - d)
+                for n in range(SUM_PARTS):
+                    pass_down(chips - 1 - d, n, True)
+
+        @pl.when(z + d < chips)
+        def _():
+            experts_of(z + d)
+
+            @pl.when(z == 0)
+            def _():
+                part_side_arrival(d)
+                for n in range(SUM_PARTS):
+                    pass_up(d, n, True)
+
+        if d + 2 < chips:
+            for part in range(HALO_PARTS + 1):
+                forward(d + 2, part)
+
+    for s in range(2, chips):
         far = chips - 1 - s
-
-        @pl.when(z < s)
-        def _():
-            expert_pair(s)
-
-        @pl.when(z == 0)
-        def _():
-            pass_up(s, True)
-
-        @pl.when(z > far)
-        def _():
-            expert_pair(far)
-
-        @pl.when(z == chips - 1)
-        def _():
-            pass_down(far, True)
-
-    expert_pair(z)
-    for s in range(chips - 1, 0, -1):
-        far = chips - 1 - s
-
-        @pl.when((z < s) & has_below)
-        def _():
-            pass_up(s, False)
-
-        @pl.when((z > far) & has_above)
-        def _():
-            pass_down(far, False)
+        goes_up = (z < s) & has_below
+        goes_down = (z > far) & has_above
+
+        @pl.when(goes_up)
+        def _():
+            part_side_arrival(s)
+
+        @pl.when(goes_down)
+        def _():
+            part_side_arrival(far)
+
+        for n in range(SUM_PARTS):
+            @pl.when(goes_up)
+            def _():
+                pass_up(s, n, False)
+
+            @pl.when(goes_down)
+            def _():
+                pass_down(far, n, False)
 
     part_side_arrival(z)
     for n in range(SUM_PARTS):

time: 163 us -> 172 us (1.055)
  the two profiles are of different devices: /device:TPU:20 before, /device:TPU:4 now
where the time goes in v3:
time: 172 us; the launch traced here: 171 us
  Pallas kernels  163 us (95%)
  local copies, waits for them, and re-layouts  4.22 us (2%)
  other arithmetic  3.47 us (2%)
    pallas_call x1, Pallas kernels, local(): pl.pallas_call(functools.partial(fused_kernel, frames, rows, features //...  163 us
    unnamed x4, local copies, waits for them, and re-layouts  3.88 us

profile of v3, /device:TPU:4, one launch (start us, length us, event | category | flops | bytes accessed | tf_op | source)
XLA Modules:
  0.0 171.2 jit_solution(11344832636285472787)
XLA Ops:
  0.0 0.1 stack.41
  0.1 0.1 stack.47
  0.2 0.7 compare_reduce_fusion.1
  0.9 0.1 broadcast_bitcast_fusion
  1.0 0.6 copy.16
  1.6 0.8 compare_reduce_fusion
  2.4 0.6 convert_element_type.5.sel
  3.0 1.2 copy.13
  4.2 0.2 pad.4
  4.3 1.3 pad_maximum_fusion.router
  5.6 163.4 %shard_map.100 = bf16[128,3072]{1,0:T(8,128)(2,1)} custom-call(bf16[128,3072]{1,0:T(8,128)(2,1)} %li.1, bf16[128,3072]{1,0:T(8,128)(2,1)} %q.1, bf16[128,3072]{1,0:T(8,128)(2,1)} %k.1, bf16[128,3072]{1,0:T(8,128)(2,1)} %v.1, f32[1,640]{1,0:T(1,128)} %bitcast.19, f32[1,3072]{1,0:T(1,128)} %bitcast.18, bf16[3072,128]{1,0:T(8,128)(2,1)} %pad_maximum_fusion.router, ...), custom_call_target="tpu_custom_call" | custom-call | tf_op jit(solution)/shard_map/pallas_call | solution.py:641
  169.1 2.1 %copy.18 = bf16[128,3072]{1,0:T(8,128)(2,1)} copy(bf16[128,3072]{1,0:T(8,128)(2,1)} %shard_map.100) | data formatting | bytes 1572864
  (2 shorter events, 0.0 us)

commit v4 on v2

--- a/solution.py
+++ b/solution.py
@@ -204,7 +204,7 @@
 
 
 HALO_PARTS = 6
-SUM_PARTS = 4
+SUM_PARTS = 8
 MESH = pl.DeviceIdType.MESH
 
 
@@ -469,27 +469,23 @@
     def part_side_arrival(t):
         part_side(t).wait_recv()
 
-    def pass_up(t, head):
-        part_side_arrival(t)
-        for n in range(SUM_PARTS):
-            piece = pl.ds(n * height, height)
-            total = p[2 * t + c, piece].astype(jnp.float32) + sib[t, piece].astype(jnp.float32)
-            if not head:
-                sum_up(t, n).wait_recv()
-                total = total + fd[t, piece].astype(jnp.float32)
-            p[2 * t + c, piece] = total.astype(jnp.bfloat16)
-            sum_up(t, n).start()
-
-    def pass_down(t, head):
-        part_side_arrival(t)
-        for n in range(SUM_PARTS):
-            piece = pl.ds(n * height, height)
-            total = p[2 * t + c, piece].astype(jnp.float32) + sib[t, piece].astype(jnp.float32)
-            if not head:
-                sum_down(t, n).wait_recv()
-                total = total + fu[t, piece].astype(jnp.float32)
-            p[2 * t + c, piece] = total.astype(jnp.bfloat16)
-            sum_down(t, n).start()
+    def pass_up(t, n, head):
+        piece = pl.ds(n * height, height)
+        total = p[2 * t + c, piece].astype(jnp.float32) + sib[t, piece].astype(jnp.float32)
+        if not head:
+            sum_up(t, n).wait_recv()
+            total = total + fd[t, piece].astype(jnp.float32)
+        p[2 * t + c, piece] = total.astype(jnp.bfloat16)
+        sum_up(t, n).start()
+
+    def pass_down(t, n, head):
+        piece = pl.ds(n * height, height)
+        total = p[2 * t + c, piece].astype(jnp.float32) + sib[t, piece].astype(jnp.float32)
+        if not head:
+            sum_down(t, n).wait_recv()
+            total = total + fu[t, piece].astype(jnp.float32)
+        p[2 * t + c, piece] = total.astype(jnp.bfloat16)
+        sum_down(t, n).start()
 
     load_up.wait()
     load_dn.wait()
@@ -506,7 +502,9 @@
 
         @pl.when(z == 0)
         def _():
-            pass_up(s, True)
+            part_side_arrival(s)
+            for n in range(SUM_PARTS):
+                pass_up(s, n, True)
 
         @pl.when(z > far)
         def _():
@@ -514,19 +512,32 @@
 
         @pl.when(z == chips - 1)
         def _():
-            pass_down(far, True)
+            part_side_arrival(far)
+            for n in range(SUM_PARTS):
+                pass_down(far, n, True)
 
     expert_pair(z)
-    for s in range(chips - 1, 0, -1):
+    for s in range(chips - 1, 1, -1):
         far = chips - 1 - s
-
-        @pl.when((z < s) & has_below)
-        def _():
-            pass_up(s, False)
-
-        @pl.when((z > far) & has_above)
-        def _():
-            pass_down(far, False)
+        goes_up = (z < s) & has_below
+        goes_down = (z > far) & has_above
+
+        @pl.when(goes_up)
+        def _():
+            part_side_arrival(s)
+
+        @pl.when(goes_down)
+        def _():
+            part_side_arrival(far)
+
+        for n in range(SUM_PARTS):
+            @pl.when(goes_up)
+            def _():
+                pass_up(s, n, False)
+
+            @pl.when(goes_down)
+            def _():
+                pass_down(far, n, False)
 
     part_side_arrival(z)
     for n in range(SUM_PARTS):

time: 163 us -> 181 us (1.11)
  the two profiles are of different devices: /device:TPU:20 before, /device:TPU:18 now
where the time goes in v4:
time: 181 us
  Pallas kernels  173 us (96%)
  local copies, waits for them, and re-layouts  4.22 us (2%)
  other arithmetic  3.47 us (2%)
    pallas_call x1, Pallas kernels, local(): pl.pallas_call(functools.partial(fused_kernel, frames, rows, features //...  173 us
    unnamed x4, local copies, waits for them, and re-layouts  3.88 us

profile of v4, /device:TPU:18, one launch (start us, length us, event | category | flops | bytes accessed | tf_op | source)
XLA Modules:
  0.0 181.0 jit_solution(16075212779020955457)
XLA Ops:
  0.0 0.1 stack.41
  0.1 0.1 stack.47
  0.2 0.7 compare_reduce_fusion.1
  0.9 0.1 broadcast_bitcast_fusion
  1.0 0.6 copy.16
  1.6 0.8 compare_reduce_fusion
  2.4 0.6 convert_element_type.5.sel
  3.0 1.2 copy.13
  4.2 0.2 pad.4
  4.3 1.3 pad_maximum_fusion.router
  5.6 173.3 %shard_map.100 = bf16[128,3072]{1,0:T(8,128)(2,1)} custom-call(bf16[128,3072]{1,0:T(8,128)(2,1)} %li.1, bf16[128,3072]{1,0:T(8,128)(2,1)} %q.1, bf16[128,3072]{1,0:T(8,128)(2,1)} %k.1, bf16[128,3072]{1,0:T(8,128)(2,1)} %v.1, f32[1,640]{1,0:T(1,128)} %bitcast.19, f32[1,3072]{1,0:T(1,128)} %bitcast.18, bf16[3072,128]{1,0:T(8,128)(2,1)} %pad_maximum_fusion.router, ...), custom_call_target="tpu_custom_call" | custom-call | tf_op jit(solution)/shard_map/pallas_call | solution.py:631
  178.9 2.1 %copy.18 = bf16[128,3072]{1,0:T(8,128)(2,1)} copy(bf16[128,3072]{1,0:T(8,128)(2,1)} %shard_map.100) | data formatting | bytes 1572864
  (2 shorter events, 0.0 us)
